TPU v7x, 256 devices: a whole 4x4x8 slice. The times are simulated.
256 devices in a mesh: row: 128 (over z, y, x_lo, core), col: 2 (over x_hi).
Axes of the slice: x: 4 (x_hi: 2, x_lo: 2; x = x_hi * 2 + x_lo), y: 4, z: 8, core: 2. Of those that a mesh axis runs over, the one named last changes fastest.
Arguments:
- tall_panel_array: float32 [128, 1048576], P('col', 'row')
- row_signs: int32 [1048576], P('row'), may hold values from -1 to 1, as said below
- sample_rows: int32 [4096], replicated, may hold values from 0 to 1048575, as said below
Outputs:
- orthobasis: float32 [128, 4096], P('col', 'row')
- triangular: float32 [128, 128], P('col')
Inputs may be any that keep to these rules, and one draw needn't show every extreme that they name: `row_signs`: each entry is -1 or +1. `sample_rows`: sketch row s keeps a panel row of the block from (s // 32) * 8192 to (s // 32 + 1) * 8192 - 1; a panel row may be kept more than once.
All inputs are finite; a program needn't handle non-finite values.
Results may differ from a plain program's by a relative error of at most 0.00016.
Values sent between devices are 32-bit elements; how exact they have to be, the bound alone decides.
A program may use at most 64 MiB of HBM per device.

v0:
```python
import jax
import jax.numpy as jnp
from jax import lax
from jax.experimental import pallas as pl
from jax.experimental.pallas import tpu as pltpu
from jax.sharding import PartitionSpec as P

F32 = jnp.float32
BF16 = jnp.bfloat16
MESH = pl.DeviceIdType.MESH
LO = 256
NU = 32
LOCAL = LO * NU
HALF = LOCAL // 2


def parity(bits):
    bits = bits ^ (bits >> 4)
    bits = bits ^ (bits >> 2)
    bits = bits ^ (bits >> 1)
    return bits & 1


def away(k):
    b = (k + 6) % 8
    return 4 + (b // 2) * (1 - 2 * (b % 2)) - b % 2 + b // 7 - k // 7


def mix_kernel(
    x_hbm, sg_hbm, idx_hbm, both_out,
    xv, sgv, idxv, idx, t, zo, acc, rc, rf, ry, rz, rx, ms, mt, gs, gr, gz, gf,
    in_sem, cs, cr, fs, fr, ys, yr, zs, zr, xs, xr, gss, gsr, gzs, gzr, gfs, gfr,
):
    row, col = lax.axis_index("row"), lax.axis_index("col")
    c = row % 2
    xl = (row // 2) % 2
    y = (row // 4) % 4
    z = row // 16
    x = col * 2 + xl

    def dev(z_, y_, x_, c_):
        return {"row": z_ * 16 + y_ * 4 + (x_ % 2) * 2 + c_, "col": x_ // 2}

    def near(dy, dx, dc):
        return dev(z, (y + dy) % 4, (x + dx) % 4, (c + dc) % 2)

    def plane(i):
        return near(i // 8, (i // 2) % 4, i % 2)

    def along_z(d):
        return dev((z + d) % 8, y, x, c)

    def loop(first, last, body):
        def step(i, carry):
            body(i)
            return carry

        lax.fori_loop(first, last, step, 0)

    fetch_rows = pltpu.make_async_copy(idx_hbm, idxv, in_sem.at[8])
    fetch_signs = pltpu.make_async_copy(sg_hbm, sgv, in_sem.at[9])
    place_rows = pltpu.make_async_copy(idxv, idx, in_sem.at[10])

    def fetch(i):
        at = pl.ds(pl.multiple_of(i * 8, 8), 8)
        return pltpu.make_async_copy(x_hbm.at[at], xv.at[at], in_sem.at[i])

    fetch_rows.start()
    fetch_signs.start()
    loop(0, 8, lambda i: fetch(i).start())

    barrier = pltpu.get_barrier_semaphore()
    loop(1, 32, lambda i: pl.semaphore_signal(barrier, inc=1, device_id=plane(i), device_id_type=MESH))
    loop(1, 8, lambda d: pl.semaphore_signal(barrier, inc=1, device_id=along_z(d), device_id_type=MESH))

    ri = lax.broadcasted_iota(jnp.int32, (LO, LO), 0)
    ci = lax.broadcasted_iota(jnp.int32, (LO, LO), 1)
    h = ((1 - 2 * parity(ri & ci)).astype(F32) * (1.0 / 1024.0)).astype(BF16)
    h = jnp.concatenate([h, h, h], axis=1)
    fetch_rows.wait()
    idxv[...] = idxv[...] & (LOCAL - 1)
    place_rows.start()
    fetch_signs.wait()

    def butterfly(i):
        fetch(i).wait()
        rows = pl.ds(pl.multiple_of(i * 8, 8), 8)
        for bt in range(LO // 128):
            v = []
            for u in range(NU):
                at = u * LO + bt * 128
                v.append(xv[rows, at : at + 128] * sgv[at // 128 : at // 128 + 1, :].astype(F32))
            step = 1
            while step < NU:
                for u in range(NU):
                    if not u & step:
                        v[u], v[u + step] = v[u] + v[u + step], v[u] - v[u + step]
                step *= 2
            for u in range(NU):
                at = u * LO + bt * 128
                xv[rows, at : at + 128] = v[u]

    loop(0, 8, butterfly)

    def lower(g):
        parts = []
        for i in range(2):
            for top in (0, NU // 2):
                at = (2 * g + i + top) * LO
                v = xv[:, at : at + LO]
                hi = v.astype(BF16)
                rest = v - hi.astype(F32)
                mid = rest.astype(BF16)
                low = (rest - mid.astype(F32)).astype(BF16)
                parts.append(jnp.concatenate([hi, mid, low], axis=1))
        w = jnp.concatenate(parts, axis=0)
        o = lax.dot_general(h, w, (((1,), (1,)), ((), ())), preferred_element_type=F32)
        for i in range(2):
            part = o[:, 128 * i : 128 * i + 128]
            at = (2 * g + i) * LO
            t[at : at + LO, :] = part
            t[at + LOCAL : at + LOCAL + LO, :] = part
            t[at + HALF : at + HALF + LO, :] = pltpu.roll(part, 64, 1)

    for g in range(NU // 4):
        lower(g)

    place_rows.wait()
    pl.semaphore_wait(barrier, 38)

    left = lax.broadcasted_iota(jnp.int32, (8, 128), 1) < 64
    sub = lax.broadcasted_iota(jnp.int32, (8, 128), 0)
    shifted = t.at[pl.ds(HALF, LOCAL)]

    def pick(out, k, cq):
        zq = (z + away(k)) % 8

        def body(i, carry):
            q = zq * 16 + i * 2 + cq
            sign = (1 - 2 * parity(row & q)).astype(F32)
            for top in (0, 8):
                v = None
                for j in range(8):
                    a = jnp.broadcast_to(t[pl.ds(idx[q * 32 + top + j], 1), :], (8, 128))
                    b = jnp.broadcast_to(shifted[pl.ds(idx[q * 32 + 16 + top + j], 1), :], (8, 128))
                    r = jnp.where(left, a, b)
                    v = r if v is None else jnp.where(sub == j, r, v)
                out[k, pl.ds(pl.multiple_of(i * 16, 16) + top, 8), :] = v * sign
            return carry

        lax.fori_loop(0, 8, body, 0, unroll=8)

    def remote(src, dst, ss, rs, device):
        return pltpu.make_async_remote_copy(
            src_ref=src, dst_ref=dst, send_sem=ss, recv_sem=rs,
            device_id=device, device_id_type=MESH,
        )

    def all_of(ref, ss, rs):
        return remote(ref, ref, ss, rs, near(0, 0, 1))

    def block(i):
        return pl.ds(pl.multiple_of(i * 32, 32), 32)

    def to_core(k):
        return remote(zo.at[k], rc.at[k], cs, cr.at[k], near(0, 0, 1))

    def to_y(k, d):
        return remote(acc.at[k, block((y + d) % 4)], ry.at[k - 2, d - 1], ys, yr.at[k - 2], near(d, 0, 0))

    def to_z(k):
        return remote(acc.at[k, block(y)], rz.at[k - 2], zs, zr, along_z(away(k)))

    def to_first(k):
        return remote(acc.at[k], rf.at[k], fs, fr, along_z(away(k)))

    def pick_other(k):
        pick(zo, k, 1 - c)
        to_core(k).start()

    def send_y(k):
        for d in (2, 1, 3):
            to_y(k, d).start()

    def pick_own(k):
        pick(acc, k, c)
        to_core(k).wait_recv()
        acc[k] = acc[k] + rc[k]
        pl.when(k < 2)(lambda: to_first(k).start())
        pl.when(k % 7 >= 2)(lambda: send_y(k))

    def add_y(k):
        all_of(ry.at[k - 2], ys, yr.at[k - 2]).wait_recv()
        mine = block(y)
        acc[k, mine] = (acc[k, mine] + ry[k - 2, 0]) + (ry[k - 2, 1] + ry[k - 2, 2])

    def pass_z(k):
        add_y(k)
        to_z(k).start()

    loop(0, 8, pick_other)
    loop(0, 8, pick_own)
    all_of(rf, fs, fr).wait_recv()
    acc[7] = acc[7] + (rf[0] + rf[1])
    send_y(7)
    loop(2, 7, pass_z)
    add_y(7)
    all_of(rz, zs, zr).wait_recv()
    rx[x] = (acc[7, block(y)] + rz[0]) + ((rz[1] + rz[2]) + (rz[3] + rz[4]))

    def to_x(d):
        return remote(rx.at[x], rx.at[x], xs, xr, near(0, d, 0))

    for d in (2, 1, 3):
        to_x(d).start()

    all_of(zo, cs, cr.at[0]).wait_send()
    all_of(rf, fs, fr).wait_send()
    all_of(ry, ys, yr.at[0]).wait_send()
    all_of(rx.at[pl.ds(0, 3)], xs, xr).wait_recv()
    a0 = rx[0] + rx[1]
    a1 = rx[2] + rx[3]
    first = jnp.concatenate([a0[:, :64], a1[:, :64]], axis=1)
    second = jnp.concatenate([a0[:, 64:], a1[:, 64:]], axis=1)
    m = jnp.concatenate([first, second], axis=0)
    mt[...] = m.T
    g = jnp.dot(
        mt[pl.ds(pl.multiple_of(x * 32, 32), 32), :], m,
        preferred_element_type=F32, precision=lax.Precision.HIGHEST,
    )
    for e in range(8):
        gs[e] = g[4 * e : 4 * e + 4]

    own = y * 2 + c

    def to_gs(i):
        dy, dc = i // 2, i % 2
        e = ((y + dy) % 4) * 2 + (c + dc) % 2
        return remote(gs.at[e], gr.at[i - 1], gss, gsr, near(dy, 0, dc))

    def to_gz(d):
        return remote(gz.at[z], gz.at[z], gzs, gzr, along_z(d))

    place = x * 8 + own

    def to_gf(i):
        return remote(gf.at[place], gf.at[place], gfs, gfr, plane(i))

    loop(1, 8, lambda i: to_gs(i).start())
    ms[0, 0], ms[0, 1] = first[:16], first[16:]
    ms[1, 0], ms[1, 1] = second[:16], second[16:]
    both_out[128:144, :] = ms[0, xl]
    both_out[144:160, :] = ms[1, xl]
    all_of(rz, zs, zr).wait_send()
    all_of(rx.at[pl.ds(0, 3)], xs, xr).wait_send()
    all_of(gr, gss, gsr).wait_recv()
    gz[z] = ((gs[own] + gr[0]) + (gr[1] + gr[2])) + ((gr[3] + gr[4]) + (gr[5] + gr[6]))
    loop(1, 8, lambda d: to_gz(d).start())
    all_of(gr, gss, gsr).wait_send()
    all_of(gz.at[pl.ds(0, 7)], gzs, gzr).wait_recv()
    gf[place] = (((gz[0] + gz[1]) + (gz[2] + gz[3])) + ((gz[4] + gz[5]) + (gz[6] + gz[7]))) * (1.0 / 4096.0)
    loop(0, 31, lambda i: to_gf((i + 19) % 31 + 1).start())
    all_of(gz.at[pl.ds(0, 7)], gzs, gzr).wait_send()
    all_of(gf.at[pl.ds(0, 31)], gfs, gfr).wait_recv()
    for e in range(32):
        both_out[e * 4 : (e + 1) * 4, :] = gf[e]
    all_of(gf.at[pl.ds(0, 31)], gfs, gfr).wait_send()


def mix(panel, signs, rows):
    vm = pl.BlockSpec(memory_space=pltpu.VMEM)
    hbm = pl.BlockSpec(memory_space=pltpu.HBM)
    V = pltpu.VMEM
    D = pltpu.SemaphoreType.DMA
    return pl.pallas_call(
        mix_kernel,
        out_shape=jax.ShapeDtypeStruct((160, 128), F32),
        in_specs=[hbm, hbm, hbm],
        out_specs=vm,
        scratch_shapes=[
            V((64, LOCAL), F32),
            V((LOCAL // 128, 128), jnp.int32),
            V((4096,), jnp.int32),
            pltpu.SMEM((4096,), jnp.int32),
            V((LOCAL + HALF, 128), F32),
            V((8, 128, 128), F32),
            V((8, 128, 128), F32),
            V((8, 128, 128), F32),
            V((2, 128, 128), F32),
            V((6, 3, 32, 128), F32),
            V((5, 32, 128), F32),
            V((4, 32, 128), F32),
            V((2, 2, 16, 128), F32),
            V((128, 64), F32),
            V((8, 4, 128), F32),
            V((7, 4, 128), F32),
            V((8, 4, 128), F32),
            V((32, 4, 128), F32),
            D((11,)),
            D, D((8,)), D, D, D, D((6,)), D, D, D, D, D, D, D, D, D, D,
        ],
        compiler_params=pltpu.CompilerParams(
            collective_id=0, has_side_effects=True, vmem_limit_bytes=62 << 20
        ),
        name="mix",
    )(panel, signs.reshape(LOCAL // 128, 128), rows)


def rows_const(v, j):
    return jnp.broadcast_to(v[:, j : j + 1], (8, 128))


def factor_kernel(both_ref, basis_ref, tri_ref, a_ref, u_ref):
    n, width = 128, 32
    col = lax.axis_index("col")
    a_ref[:, :128] = both_ref[:128, :]
    samples = jnp.concatenate([both_ref[128:, :], jnp.zeros((96, 128), F32)], axis=0)
    a_ref[:, 128:] = samples.T
    lane = lax.broadcasted_iota(jnp.int32, (8, 128), 1)
    for panel in range(n // width):
        top = panel * width
        nb = width // 8
        blocks = [
            [a_ref[top + 8 * i : top + 8 * i + 8, 128 * t : 128 * t + 128] for t in range(2)]
            for i in range(nb)
        ]
        for j in range(nb):
            at = top + 8 * j
            rows = [
                [jnp.broadcast_to(blocks[j][t][k : k + 1, :], (8, 128)) for t in range(2)]
                for k in range(8)
            ]
            d = {(i, k): rows_const(rows[i][0], at + k) for i in range(8) for k in range(i + 1)}
            below = [[rows_const(blocks[i][0], at + k) for k in range(8)] for i in range(j + 1, nb)]
            for k in range(8):
                r = lax.rsqrt(d[k, k])
                for i in range(k + 1, 8):
                    d[i, k] = d[i, k] * r
                for i in range(k + 1, 8):
                    for q in range(k + 1, i + 1):
                        d[i, q] = d[i, q] - d[i, k] * d[q, k]
                for t in range(2):
                    rows[k][t] = rows[k][t] * r
                    for q in range(k + 1, 8):
                        rows[q][t] = rows[q][t] - d[q, k] * rows[k][t]
                for b in below:
                    b[k] = b[k] * r
                    for q in range(k + 1, 8):
                        b[q] = b[q] - d[q, k] * b[k]
            for k in range(8):
                keep = lane >= at + k
                u_ref[at + k : at + k + 1, :128] = jnp.where(keep, rows[k][0], 0.0)[:1]
                u_ref[at + k : at + k + 1, 128:] = rows[k][1][:1]
            for i in range(j + 1, nb):
                b = below[i - j - 1]
                for t in range(2):
                    v = blocks[i][t]
                    for k in range(8):
                        v = v - b[k] * rows[k][t]
                    blocks[i][t] = v
        if top + width < n:
            rest = top + width
            u = u_ref[top:rest, :]
            left = u[:, :128].T[rest:, :]
            upd = jnp.dot(left, u, preferred_element_type=F32, precision=lax.Precision.HIGHEST)
            a_ref[rest:, :] = a_ref[rest:, :] - upd
    half = pl.ds(pl.multiple_of(col * 64, 64), 64)
    tri_ref[...] = u_ref[half, :128]
    basis_ref[...] = u_ref[half, 128:].T[:32]


def factor(both):
    vm = pl.BlockSpec(memory_space=pltpu.VMEM)
    return pl.pallas_call(
        factor_kernel,
        out_shape=(jax.ShapeDtypeStruct((32, 64), F32), jax.ShapeDtypeStruct((64, 128), F32)),
        in_specs=[vm],
        out_specs=(vm, vm),
        scratch_shapes=[pltpu.VMEM((128, 256), F32), pltpu.VMEM((128, 256), F32)],
        compiler_params=pltpu.CompilerParams(vmem_limit_bytes=16 << 20),
        name="factor",
    )(both)


def shards(tall_panel_array, row_signs, sample_rows):
    basis, upper = factor(mix(tall_panel_array, row_signs, sample_rows))
    return basis.T, upper


def solution(mesh):
    return jax.shard_map(
        shards,
        mesh=mesh,
        in_specs=(P("col", "row"), P("row"), P()),
        out_specs=(P("col", "row"), P("col", None)),
        check_vma=False,
    )
```

profile of v0, /device:TPU:1, one launch (start us, length us, event | category | flops | bytes accessed | tf_op | source)
XLA Modules:
  0.0 48.8 jit_solution(10433933838510788954)
XLA Ops:
  0.6 42.5 %mix.1.both_ref = f32[160,128]{1,0:T(8,128)} custom-call(f32[64,8192]{1,0:T(8,128)} %x_hbm.1, s32[64,128]{1,0:T(8,128)} %bitcast.2, s32[4096]{0:T(1024)} %idx_hbm.1), custom_call_target="tpu_custom_call" | custom-call | tf_op jit(solution)/shard_map/mix/pallas_call | solution.py:275
  43.1 0.0 copy-start
  43.1 0.9 %copy-done = f32[160,128]{1,0:T(8,128)S(1)} copy-done((f32[160,128]{1,0:T(8,128)S(1)}, f32[160,128]{1,0:T(8,128)}, u32[]{:S(2)}) %copy-start) | copy-done | bytes 81944
  44.0 4.8 %factor.1 = (f32[32,64]{1,0:T(8,128)}, f32[64,128]{1,0:T(8,128)}) custom-call(f32[160,128]{1,0:T(8,128)S(1)} %copy-done), custom_call_target="tpu_custom_call" | custom-call | tf_op jit(solution)/shard_map/factor/pallas_call | solution.py:374
Async XLA Ops:
  43.1 0.9 %copy-start = (f32[160,128]{1,0:T(8,128)S(1)}, f32[160,128]{1,0:T(8,128)}, u32[]{:S(2)}) copy-start(f32[160,128]{1,0:T(8,128)} %mix.1.both_ref) | copy-start | bytes 245764
where the time goes:
time: 48.9 us; the launch traced here: 48.8 us
  Pallas kernels  47.3 us (97%)
  local copies, waits for them, and re-layouts  0.88 us (2%)
  between operations  0.65 us (1%)
    pallas_call x1, Pallas kernels, mix(): pl.pallas_call(mix_kernel, out_shape=jax.ShapeDtypeStruct((160, 128), F32...  42.5 us
    pallas_call x1, Pallas kernels, factor(): pl.pallas_call(factor_kernel, out_shape=(jax.ShapeDtypeStruct((32, 64), F...  4.8 us

commit v1 on v0

--- a/solution.py
+++ b/solution.py
@@ -28,7 +28,7 @@
 
 def mix_kernel(
     x_hbm, sg_hbm, idx_hbm, both_out,
-    xv, sgv, idxv, idx, t, zo, acc, rc, rf, ry, rz, rx, ms, mt, gs, gr, gz, gf,
+    xv, sgv, idxv, idx, t, zo, acc, rc, rf, ry, rz, mx, gs, gr, gz, gf,
     in_sem, cs, cr, fs, fr, ys, yr, zs, zr, xs, xr, gss, gsr, gzs, gzr, gfs, gfr,
 ):
     row, col = lax.axis_index("row"), lax.axis_index("col")
@@ -72,6 +72,12 @@
     barrier = pltpu.get_barrier_semaphore()
     loop(1, 32, lambda i: pl.semaphore_signal(barrier, inc=1, device_id=plane(i), device_id_type=MESH))
     loop(1, 8, lambda d: pl.semaphore_signal(barrier, inc=1, device_id=along_z(d), device_id_type=MESH))
+
+    def greet_line(i):
+        d = dev((z + 2 + i // 3) % 8, y, (x + 1 + i % 3) % 4, c)
+        pl.semaphore_signal(barrier, inc=1, device_id=d, device_id_type=MESH)
+
+    loop(0, 15, greet_line)
 
     ri = lax.broadcasted_iota(jnp.int32, (LO, LO), 0)
     ci = lax.broadcasted_iota(jnp.int32, (LO, LO), 1)
@@ -126,7 +132,7 @@
         lower(g)
 
     place_rows.wait()
-    pl.semaphore_wait(barrier, 38)
+    pl.semaphore_wait(barrier, 53)
 
     left = lax.broadcasted_iota(jnp.int32, (8, 128), 1) < 64
     sub = lax.broadcasted_iota(jnp.int32, (8, 128), 0)
@@ -168,8 +174,11 @@
     def to_y(k, d):
         return remote(acc.at[k, block((y + d) % 4)], ry.at[k - 2, d - 1], ys, yr.at[k - 2], near(d, 0, 0))
 
-    def to_z(k):
-        return remote(acc.at[k, block(y)], rz.at[k - 2], zs, zr, along_z(away(k)))
+    def quarter(k, i):
+        return acc.at[k, pl.ds(pl.multiple_of(y * 32 + (i % 2) * 16 + (i // 2) * 8, 8), 8)]
+
+    def to_z(k, i):
+        return remote(quarter(k, i), rz.at[(k - 2) * 4 + x], zs, zr, dev((z + away(k)) % 8, y, i, c))
 
     def to_first(k):
         return remote(acc.at[k], rf.at[k], fs, fr, along_z(away(k)))
@@ -196,7 +205,8 @@
 
     def pass_z(k):
         add_y(k)
-        to_z(k).start()
+        for i in range(4):
+            to_z(k, i).start()
 
     loop(0, 8, pick_other)
     loop(0, 8, pick_own)
@@ -205,58 +215,58 @@
     send_y(7)
     loop(2, 7, pass_z)
     add_y(7)
-    all_of(rz, zs, zr).wait_recv()
-    rx[x] = (acc[7, block(y)] + rz[0]) + ((rz[1] + rz[2]) + (rz[3] + rz[4]))
-
-    def to_x(d):
-        return remote(rx.at[x], rx.at[x], xs, xr, near(0, d, 0))
-
     for d in (2, 1, 3):
-        to_x(d).start()
-
+        to_z(7, (x + d) % 4).start()
+    rz[20 + x] = quarter(7, x)[...]
     all_of(zo, cs, cr.at[0]).wait_send()
     all_of(rf, fs, fr).wait_send()
     all_of(ry, ys, yr.at[0]).wait_send()
-    all_of(rx.at[pl.ds(0, 3)], xs, xr).wait_recv()
-    a0 = rx[0] + rx[1]
-    a1 = rx[2] + rx[3]
+    others = all_of(rz.at[pl.ds(0, 23)], zs, zr)
+    others.wait_recv()
+
+    def total(i):
+        v = [rz[4 * k + i] for k in range(6)] + [rz[4 * k + i + 1] for k in range(6)]
+        while len(v) > 1:
+            v = [v[j] + v[j + 1] if j + 1 < len(v) else v[j] for j in range(0, len(v), 2)]
+        return v[0]
+
+    a0, a1 = total(0), total(2)
     first = jnp.concatenate([a0[:, :64], a1[:, :64]], axis=1)
     second = jnp.concatenate([a0[:, 64:], a1[:, 64:]], axis=1)
     m = jnp.concatenate([first, second], axis=0)
-    mt[...] = m.T
-    g = jnp.dot(
-        mt[pl.ds(pl.multiple_of(x * 32, 32), 32), :], m,
-        preferred_element_type=F32, precision=lax.Precision.HIGHEST,
-    )
-    for e in range(8):
+    g = jnp.dot(m.T, m, preferred_element_type=F32, precision=lax.Precision.HIGHEST)
+    for e in range(32):
         gs[e] = g[4 * e : 4 * e + 4]
 
-    own = y * 2 + c
+    place = x * 8 + y * 2 + c
 
     def to_gs(i):
-        dy, dc = i // 2, i % 2
-        e = ((y + dy) % 4) * 2 + (c + dc) % 2
-        return remote(gs.at[e], gr.at[i - 1], gss, gsr, near(dy, 0, dc))
+        e = ((x + (i // 2) % 4) % 4) * 8 + ((y + i // 8) % 4) * 2 + (c + i % 2) % 2
+        return remote(gs.at[e], gr.at[i - 1], gss, gsr, plane(i))
+
+    to_mate = remote(mx.at[x // 2], mx.at[x // 2], xs, xr, near(0, 2, 0))
 
     def to_gz(d):
         return remote(gz.at[z], gz.at[z], gzs, gzr, along_z(d))
 
-    place = x * 8 + own
-
     def to_gf(i):
         return remote(gf.at[place], gf.at[place], gfs, gfr, plane(i))
 
-    loop(1, 8, lambda i: to_gs(i).start())
-    ms[0, 0], ms[0, 1] = first[:16], first[16:]
-    ms[1, 0], ms[1, 1] = second[:16], second[16:]
-    both_out[128:144, :] = ms[0, xl]
-    both_out[144:160, :] = ms[1, xl]
-    all_of(rz, zs, zr).wait_send()
-    all_of(rx.at[pl.ds(0, 3)], xs, xr).wait_send()
+    loop(0, 31, lambda i: to_gs((i + 19) % 31 + 1).start())
+    mx[x // 2] = m
+    to_mate.start()
+    others.wait_send()
     all_of(gr, gss, gsr).wait_recv()
-    gz[z] = ((gs[own] + gr[0]) + (gr[1] + gr[2])) + ((gr[3] + gr[4]) + (gr[5] + gr[6]))
+    v = [gr[i] for i in range(31)] + [gs[place]]
+    while len(v) > 1:
+        v = [v[j] + v[j + 1] for j in range(0, len(v), 2)]
+    gz[z] = v[0]
     loop(1, 8, lambda d: to_gz(d).start())
     all_of(gr, gss, gsr).wait_send()
+    to_mate.wait()
+    for i in range(2):
+        for j in range(2):
+            both_out[128 + 16 * j + 8 * i : 136 + 16 * j + 8 * i, :] = mx[i, 8 * j : 8 * j + 8]
     all_of(gz.at[pl.ds(0, 7)], gzs, gzr).wait_recv()
     gf[place] = (((gz[0] + gz[1]) + (gz[2] + gz[3])) + ((gz[4] + gz[5]) + (gz[6] + gz[7]))) * (1.0 / 4096.0)
     loop(0, 31, lambda i: to_gf((i + 19) % 31 + 1).start())
@@ -288,12 +298,10 @@
             V((8, 128, 128), F32),
             V((2, 128, 128), F32),
             V((6, 3, 32, 128), F32),
-            V((5, 32, 128), F32),
-            V((4, 32, 128), F32),
-            V((2, 2, 16, 128), F32),
-            V((128, 64), F32),
-            V((8, 4, 128), F32),
-            V((7, 4, 128), F32),
+            V((24, 8, 128), F32),
+            V((2, 16, 128), F32),
+            V((32, 4, 128), F32),
+            V((31, 4, 128), F32),
             V((8, 4, 128), F32),
             V((32, 4, 128), F32),
             D((11,)),

time: 48.9 us -> 50.1 us (1.025)
  Pallas kernels: 47.3 us -> 48.5 us
    pallas_call x1, Pallas kernels: 42.5 us -> 43.7 us  [mix(): pl.pallas_call(mix_kernel, out_shape=jax.ShapeDtypeStruct((160, 128), F32...]
where the time goes in v1:
time: 50.1 us; the launch traced here: 50 us
  Pallas kernels  48.5 us (97%)
  local copies, waits for them, and re-layouts  0.88 us (2%)
  between operations  0.65 us (1%)
    pallas_call x1, Pallas kernels, mix(): pl.pallas_call(mix_kernel, out_shape=jax.ShapeDtypeStruct((160, 128), F32...  43.7 us
    pallas_call x1, Pallas kernels, factor(): pl.pallas_call(factor_kernel, out_shape=(jax.ShapeDtypeStruct((32, 64), F...  4.8 us

profile of v1, /device:TPU:1, one launch (start us, length us, event | category | flops | bytes accessed | tf_op | source)
XLA Modules:
  0.0 50.0 jit_solution(11023984424298181398)
XLA Ops:
  0.6 43.7 %mix.1.both_ref = f32[160,128]{1,0:T(8,128)} custom-call(f32[64,8192]{1,0:T(8,128)} %x_hbm.1, s32[64,128]{1,0:T(8,128)} %bitcast.2, s32[4096]{0:T(1024)} %idx_hbm.1), custom_call_target="tpu_custom_call" | custom-call | tf_op jit(solution)/shard_map/mix/pallas_call | solution.py:285
  44.3 0.0 copy-start
  44.4 0.9 %copy-done = f32[160,128]{1,0:T(8,128)S(1)} copy-done((f32[160,128]{1,0:T(8,128)S(1)}, f32[160,128]{1,0:T(8,128)}, u32[]{:S(2)}) %copy-start) | copy-done | bytes 81944
  45.2 4.8 %factor.1 = (f32[32,64]{1,0:T(8,128)}, f32[64,128]{1,0:T(8,128)}) custom-call(f32[160,128]{1,0:T(8,128)S(1)} %copy-done), custom_call_target="tpu_custom_call" | custom-call | tf_op jit(solution)/shard_map/factor/pallas_call | solution.py:382
Async XLA Ops:
  44.3 0.9 %copy-start = (f32[160,128]{1,0:T(8,128)S(1)}, f32[160,128]{1,0:T(8,128)}, u32[]{:S(2)}) copy-start(f32[160,128]{1,0:T(8,128)} %mix.1.both_ref) | copy-start | bytes 245764

commit v2 on v0

--- a/solution.py
+++ b/solution.py
@@ -32,23 +32,26 @@
     in_sem, cs, cr, fs, fr, ys, yr, zs, zr, xs, xr, gss, gsr, gzs, gzr, gfs, gfr,
 ):
     row, col = lax.axis_index("row"), lax.axis_index("col")
-    c = row % 2
-    xl = (row // 2) % 2
-    y = (row // 4) % 4
-    z = row // 16
+    c = row & 1
+    xl = (row >> 1) & 1
+    y = (row >> 2) & 3
+    z = row >> 4
     x = col * 2 + xl
 
-    def dev(z_, y_, x_, c_):
-        return {"row": z_ * 16 + y_ * 4 + (x_ % 2) * 2 + c_, "col": x_ // 2}
-
-    def near(dy, dx, dc):
-        return dev(z, (y + dy) % 4, (x + dx) % 4, (c + dc) % 2)
-
-    def plane(i):
-        return near(i // 8, (i // 2) % 4, i % 2)
+    y_at = [((y + d) & 3) * 4 for d in range(4)]
+    x_at = [(((x + d) & 1) * 2, ((x + d) & 3) >> 1) for d in range(4)]
+    c_at = [c, 1 - c]
+    z_at = [((z + d) & 7) * 16 for d in range(8)]
+
+    def near(dy, dx, dc, dz=0):
+        return {"row": z_at[dz] + y_at[dy] + x_at[dx][0] + c_at[dc], "col": x_at[dx][1]}
 
     def along_z(d):
-        return dev((z + d) % 8, y, x, c)
+        return {"row": ((z + d) & 7) * 16 + (row & 15), "col": col}
+
+    plane = [(dy, dx, dc) for dy in (2, 1, 3, 0) for dx in (2, 1, 3, 0) for dc in (1, 0) if dy or dx or dc]
+    part = [(dy, 0, dc) for dy in (2, 1, 3, 0) for dc in (1, 0) if dy or dc]
+    z_order = (4, 3, 5, 2, 6, 1, 7)
 
     def loop(first, last, body):
         def step(i, carry):
@@ -70,8 +73,8 @@
     loop(0, 8, lambda i: fetch(i).start())
 
     barrier = pltpu.get_barrier_semaphore()
-    loop(1, 32, lambda i: pl.semaphore_signal(barrier, inc=1, device_id=plane(i), device_id_type=MESH))
-    loop(1, 8, lambda d: pl.semaphore_signal(barrier, inc=1, device_id=along_z(d), device_id_type=MESH))
+    for d in [near(*i) for i in plane] + [near(0, 0, 0, d) for d in z_order]:
+        pl.semaphore_signal(barrier, inc=1, device_id=d, device_id_type=MESH)
 
     ri = lax.broadcasted_iota(jnp.int32, (LO, LO), 0)
     ci = lax.broadcasted_iota(jnp.int32, (LO, LO), 1)
@@ -133,7 +136,7 @@
     shifted = t.at[pl.ds(HALF, LOCAL)]
 
     def pick(out, k, cq):
-        zq = (z + away(k)) % 8
+        zq = (z + away(k)) & 7
 
         def body(i, carry):
             q = zq * 16 + i * 2 + cq
@@ -166,7 +169,7 @@
         return remote(zo.at[k], rc.at[k], cs, cr.at[k], near(0, 0, 1))
 
     def to_y(k, d):
-        return remote(acc.at[k, block((y + d) % 4)], ry.at[k - 2, d - 1], ys, yr.at[k - 2], near(d, 0, 0))
+        return remote(acc.at[k, block((y + d) & 3)], ry.at[k - 2, d - 1], ys, yr.at[k - 2], near(d, 0, 0))
 
     def to_z(k):
         return remote(acc.at[k, block(y)], rz.at[k - 2], zs, zr, along_z(away(k)))
@@ -234,19 +237,19 @@
     own = y * 2 + c
 
     def to_gs(i):
-        dy, dc = i // 2, i % 2
-        e = ((y + dy) % 4) * 2 + (c + dc) % 2
-        return remote(gs.at[e], gr.at[i - 1], gss, gsr, near(dy, 0, dc))
+        dy, _, dc = part[i]
+        return remote(gs.at[((y + dy) & 3) * 2 + c_at[dc]], gr.at[i], gss, gsr, near(dy, 0, dc))
 
     def to_gz(d):
-        return remote(gz.at[z], gz.at[z], gzs, gzr, along_z(d))
+        return remote(gz.at[z], gz.at[z], gzs, gzr, near(0, 0, 0, d))
 
     place = x * 8 + own
 
     def to_gf(i):
-        return remote(gf.at[place], gf.at[place], gfs, gfr, plane(i))
-
-    loop(1, 8, lambda i: to_gs(i).start())
+        return remote(gf.at[place], gf.at[place], gfs, gfr, near(*plane[i]))
+
+    for i in range(7):
+        to_gs(i).start()
     ms[0, 0], ms[0, 1] = first[:16], first[16:]
     ms[1, 0], ms[1, 1] = second[:16], second[16:]
     both_out[128:144, :] = ms[0, xl]
@@ -255,11 +258,13 @@
     all_of(rx.at[pl.ds(0, 3)], xs, xr).wait_send()
     all_of(gr, gss, gsr).wait_recv()
     gz[z] = ((gs[own] + gr[0]) + (gr[1] + gr[2])) + ((gr[3] + gr[4]) + (gr[5] + gr[6]))
-    loop(1, 8, lambda d: to_gz(d).start())
+    for d in z_order:
+        to_gz(d).start()
     all_of(gr, gss, gsr).wait_send()
     all_of(gz.at[pl.ds(0, 7)], gzs, gzr).wait_recv()
     gf[place] = (((gz[0] + gz[1]) + (gz[2] + gz[3])) + ((gz[4] + gz[5]) + (gz[6] + gz[7]))) * (1.0 / 4096.0)
-    loop(0, 31, lambda i: to_gf((i + 19) % 31 + 1).start())
+    for i in range(31):
+        to_gf(i).start()
     all_of(gz.at[pl.ds(0, 7)], gzs, gzr).wait_send()
     all_of(gf.at[pl.ds(0, 31)], gfs, gfr).wait_recv()
     for e in range(32):

time: 48.9 us -> 47.1 us (0.963)
  Pallas kernels: 47.3 us -> 45.4 us
    pallas_call x1, Pallas kernels: 42.5 us -> 40.6 us  [mix(): pl.pallas_call(mix_kernel, out_shape=jax.ShapeDtypeStruct((160, 128), F32...]
where the time goes in v2:
time: 47.1 us; the launch traced here: 46.9 us
  Pallas kernels  45.4 us (96%)
  local copies, waits for them, and re-layouts  0.88 us (2%)
  between operations  0.65 us (1%)
    pallas_call x1, Pallas kernels, mix(): pl.pallas_call(mix_kernel, out_shape=jax.ShapeDtypeStruct((160, 128), F32...  40.6 us
    pallas_call x1, Pallas kernels, factor(): pl.pallas_call(factor_kernel, out_shape=(jax.ShapeDtypeStruct((32, 64), F...  4.79 us

profile of v2, /device:TPU:1, one launch (start us, length us, event | category | flops | bytes accessed | tf_op | source)
XLA Modules:
  0.0 46.9 jit_solution(409071804177259459)
XLA Ops:
  0.6 40.6 %mix.1.both_ref = f32[160,128]{1,0:T(8,128)} custom-call(f32[64,8192]{1,0:T(8,128)} %x_hbm.1, s32[64,128]{1,0:T(8,128)} %bitcast.2, s32[4096]{0:T(1024)} %idx_hbm.1), custom_call_target="tpu_custom_call" | custom-call | tf_op jit(solution)/shard_map/mix/pallas_call | solution.py:280
  41.2 0.0 copy-start
  41.3 0.9 %copy-done = f32[160,128]{1,0:T(8,128)S(1)} copy-done((f32[160,128]{1,0:T(8,128)S(1)}, f32[160,128]{1,0:T(8,128)}, u32[]{:S(2)}) %copy-start) | copy-done | bytes 81944
  42.1 4.8 %factor.1 = (f32[32,64]{1,0:T(8,128)}, f32[64,128]{1,0:T(8,128)}) custom-call(f32[160,128]{1,0:T(8,128)S(1)} %copy-done), custom_call_target="tpu_custom_call" | custom-call | tf_op jit(solution)/shard_map/factor/pallas_call | solution.py:379
Async XLA Ops:
  41.2 0.9 %copy-start = (f32[160,128]{1,0:T(8,128)S(1)}, f32[160,128]{1,0:T(8,128)}, u32[]{:S(2)}) copy-start(f32[160,128]{1,0:T(8,128)} %mix.1.both_ref) | copy-start | bytes 245764

commit v3 on v2

--- a/solution.py
+++ b/solution.py
@@ -22,12 +22,12 @@
 
 
 def away(k):
-    b = (k + 6) % 8
-    return 4 + (b // 2) * (1 - 2 * (b % 2)) - b % 2 + b // 7 - k // 7
+    b = (k + 6) & 7
+    return 4 + (b >> 1) * (1 - 2 * (b & 1)) - (b & 1) + ((b + 1) >> 3) - ((k + 1) >> 3)
 
 
 def mix_kernel(
-    x_hbm, sg_hbm, idx_hbm, both_out,
+    x_hbm, ints, both_out,
     xv, sgv, idxv, idx, t, zo, acc, rc, rf, ry, rz, rx, ms, mt, gs, gr, gz, gf,
     in_sem, cs, cr, fs, fr, ys, yr, zs, zr, xs, xr, gss, gsr, gzs, gzr, gfs, gfr,
 ):
@@ -60,17 +60,16 @@
 
         lax.fori_loop(first, last, step, 0)
 
-    fetch_rows = pltpu.make_async_copy(idx_hbm, idxv, in_sem.at[8])
-    fetch_signs = pltpu.make_async_copy(sg_hbm, sgv, in_sem.at[9])
-    place_rows = pltpu.make_async_copy(idxv, idx, in_sem.at[10])
+    place_rows = pltpu.make_async_copy(idxv, idx, in_sem.at[8])
 
     def fetch(i):
         at = pl.ds(pl.multiple_of(i * 8, 8), 8)
         return pltpu.make_async_copy(x_hbm.at[at], xv.at[at], in_sem.at[i])
 
-    fetch_rows.start()
-    fetch_signs.start()
     loop(0, 8, lambda i: fetch(i).start())
+    idxv[...] = ints[pl.ds(LOCAL, 4096)] & (LOCAL - 1)
+    place_rows.start()
+    sgv[...] = ints[pl.ds(0, LOCAL)].reshape(LOCAL // 128, 128).astype(F32)
 
     barrier = pltpu.get_barrier_semaphore()
     for d in [near(*i) for i in plane] + [near(0, 0, 0, d) for d in z_order]:
@@ -80,10 +79,6 @@
     ci = lax.broadcasted_iota(jnp.int32, (LO, LO), 1)
     h = ((1 - 2 * parity(ri & ci)).astype(F32) * (1.0 / 1024.0)).astype(BF16)
     h = jnp.concatenate([h, h, h], axis=1)
-    fetch_rows.wait()
-    idxv[...] = idxv[...] & (LOCAL - 1)
-    place_rows.start()
-    fetch_signs.wait()
 
     def butterfly(i):
         fetch(i).wait()
@@ -92,7 +87,7 @@
             v = []
             for u in range(NU):
                 at = u * LO + bt * 128
-                v.append(xv[rows, at : at + 128] * sgv[at // 128 : at // 128 + 1, :].astype(F32))
+                v.append(xv[rows, at : at + 128] * sgv[at // 128 : at // 128 + 1, :])
             step = 1
             while step < NU:
                 for u in range(NU):
@@ -190,7 +185,7 @@
         to_core(k).wait_recv()
         acc[k] = acc[k] + rc[k]
         pl.when(k < 2)(lambda: to_first(k).start())
-        pl.when(k % 7 >= 2)(lambda: send_y(k))
+        pl.when((k >= 2) & (k < 7))(lambda: send_y(k))
 
     def add_y(k):
         all_of(ry.at[k - 2], ys, yr.at[k - 2]).wait_recv()
@@ -280,11 +275,11 @@
     return pl.pallas_call(
         mix_kernel,
         out_shape=jax.ShapeDtypeStruct((160, 128), F32),
-        in_specs=[hbm, hbm, hbm],
+        in_specs=[hbm, vm],
         out_specs=vm,
         scratch_shapes=[
             V((64, LOCAL), F32),
-            V((LOCAL // 128, 128), jnp.int32),
+            V((LOCAL // 128, 128), F32),
             V((4096,), jnp.int32),
             pltpu.SMEM((4096,), jnp.int32),
             V((LOCAL + HALF, 128), F32),
@@ -301,14 +296,14 @@
             V((7, 4, 128), F32),
             V((8, 4, 128), F32),
             V((32, 4, 128), F32),
-            D((11,)),
+            D((9,)),
             D, D((8,)), D, D, D, D((6,)), D, D, D, D, D, D, D, D, D, D,
         ],
         compiler_params=pltpu.CompilerParams(
-            collective_id=0, has_side_effects=True, vmem_limit_bytes=62 << 20
+            collective_id=0, has_side_effects=True, vmem_limit_bytes=52 << 20
         ),
         name="mix",
-    )(panel, signs.reshape(LOCAL // 128, 128), rows)
+    )(panel, jnp.concatenate([signs, rows]))
 
 
 def rows_const(v, j):

time: 47.1 us -> 46 us (0.977)
  Pallas kernels: 45.4 us -> 44.4 us
  local copies, waits for them, and re-layouts: 0.88 us -> 0 us
  other arithmetic: 0 us -> 0.78 us
    pallas_call x1, Pallas kernels: 40.6 us -> 39.6 us  [mix(): pl.pallas_call(mix_kernel, out_shape=jax.ShapeDtypeStruct((160, 128), F32...]
    unnamed x2 -> x0, local copies, waits for them, and re-layouts: 0.88 us -> none
    concatenate x0 -> x1, other arithmetic: none -> 0.78 us  [mix(): jnp.concatenate([signs, rows])]
where the time goes in v3:
time: 46 us; the launch traced here: 45.8 us
  Pallas kernels  44.4 us (97%)
  other arithmetic  0.78 us (2%)
  between operations  0.64 us (1%)
    pallas_call x1, Pallas kernels, mix(): pl.pallas_call(mix_kernel, out_shape=jax.ShapeDtypeStruct((160, 128), F32...  39.6 us
    pallas_call x1, Pallas kernels, factor(): pl.pallas_call(factor_kernel, out_shape=(jax.ShapeDtypeStruct((32, 64), F...  4.8 us

profile of v3, /device:TPU:1, one launch (start us, length us, event | category | flops | bytes accessed | tf_op | source)
XLA Modules:
  0.0 45.8 jit_solution(13601883980273211290)
XLA Ops:
  0.6 0.8 %pad_add_fusion.ints = s32[12288]{0:T(1024)S(1)} fusion(s32[4096]{0:T(1024)} %param.5, s32[8192]{0:T(1024)} %param.4), kind=kLoop, calls=%fused_computation | loop fusion | flops 12288 | bytes 98304 | tf_op jit(solution)/shard_map/concatenate | solution.py:306
  1.4 39.6 %mix.1.both_ref = f32[160,128]{1,0:T(8,128)S(1)} custom-call(f32[64,8192]{1,0:T(8,128)} %x_hbm.1, s32[12288]{0:T(1024)S(1)} %pad_add_fusion.ints), custom_call_target="tpu_custom_call" | custom-call | tf_op jit(solution)/shard_map/mix/pallas_call | solution.py:275
  41.0 4.8 %factor.1 = (f32[32,64]{1,0:T(8,128)}, f32[64,128]{1,0:T(8,128)}) custom-call(f32[160,128]{1,0:T(8,128)S(1)} %mix.1.both_ref), custom_call_target="tpu_custom_call" | custom-call | tf_op jit(solution)/shard_map/factor/pallas_call | solution.py:374

commit v4 on v3

--- a/solution.py
+++ b/solution.py
@@ -28,15 +28,14 @@
 
 def mix_kernel(
     x_hbm, ints, both_out,
-    xv, sgv, idxv, idx, t, zo, acc, rc, rf, ry, rz, rx, ms, mt, gs, gr, gz, gf,
+    xv, sgv, idxv, idx, t, zo, acc, rc, rf, ry, rz, mx, gs, gr, gz, gf,
     in_sem, cs, cr, fs, fr, ys, yr, zs, zr, xs, xr, gss, gsr, gzs, gzr, gfs, gfr,
 ):
     row, col = lax.axis_index("row"), lax.axis_index("col")
     c = row & 1
-    xl = (row >> 1) & 1
     y = (row >> 2) & 3
     z = row >> 4
-    x = col * 2 + xl
+    x = col * 2 + ((row >> 1) & 1)
 
     y_at = [((y + d) & 3) * 4 for d in range(4)]
     x_at = [(((x + d) & 1) * 2, ((x + d) & 3) >> 1) for d in range(4)]
@@ -50,7 +49,6 @@
         return {"row": ((z + d) & 7) * 16 + (row & 15), "col": col}
 
     plane = [(dy, dx, dc) for dy in (2, 1, 3, 0) for dx in (2, 1, 3, 0) for dc in (1, 0) if dy or dx or dc]
-    part = [(dy, 0, dc) for dy in (2, 1, 3, 0) for dc in (1, 0) if dy or dc]
     z_order = (4, 3, 5, 2, 6, 1, 7)
 
     def loop(first, last, body):
@@ -72,7 +70,7 @@
     sgv[...] = ints[pl.ds(0, LOCAL)].reshape(LOCAL // 128, 128).astype(F32)
 
     barrier = pltpu.get_barrier_semaphore()
-    for d in [near(*i) for i in plane] + [near(0, 0, 0, d) for d in z_order]:
+    for d in [near(*i) for i in plane] + [near(0, i, 0, d) for d in z_order for i in range(4 if 1 < d < 7 else 1)]:
         pl.semaphore_signal(barrier, inc=1, device_id=d, device_id_type=MESH)
 
     ri = lax.broadcasted_iota(jnp.int32, (LO, LO), 0)
@@ -124,7 +122,7 @@
         lower(g)
 
     place_rows.wait()
-    pl.semaphore_wait(barrier, 38)
+    pl.semaphore_wait(barrier, 53)
 
     left = lax.broadcasted_iota(jnp.int32, (8, 128), 1) < 64
     sub = lax.broadcasted_iota(jnp.int32, (8, 128), 0)
@@ -166,8 +164,12 @@
     def to_y(k, d):
         return remote(acc.at[k, block((y + d) & 3)], ry.at[k - 2, d - 1], ys, yr.at[k - 2], near(d, 0, 0))
 
-    def to_z(k):
-        return remote(acc.at[k, block(y)], rz.at[k - 2], zs, zr, along_z(away(k)))
+    def quarter(k, i):
+        return acc.at[k, pl.ds(pl.multiple_of(y * 32 + (i & 1) * 16 + (i >> 1) * 8, 8), 8)]
+
+    def to_z(k, zq, d):
+        device = {"row": zq * 16 + y_at[0] + x_at[d][0] + c, "col": x_at[d][1]}
+        return remote(quarter(k, (x + d) & 3), rz.at[(k - 2) * 4 + x], zs, zr, device)
 
     def to_first(k):
         return remote(acc.at[k], rf.at[k], fs, fr, along_z(away(k)))
@@ -194,7 +196,9 @@
 
     def pass_z(k):
         add_y(k)
-        to_z(k).start()
+        zq = (z + away(k)) & 7
+        for d in (2, 1, 3, 0):
+            to_z(k, zq, d).start()
 
     loop(0, 8, pick_other)
     loop(0, 8, pick_own)
@@ -203,59 +207,61 @@
     send_y(7)
     loop(2, 7, pass_z)
     add_y(7)
-    all_of(rz, zs, zr).wait_recv()
-    rx[x] = (acc[7, block(y)] + rz[0]) + ((rz[1] + rz[2]) + (rz[3] + rz[4]))
-
-    def to_x(d):
-        return remote(rx.at[x], rx.at[x], xs, xr, near(0, d, 0))
-
     for d in (2, 1, 3):
-        to_x(d).start()
-
+        to_z(7, z, d).start()
+    rz[20 + x] = quarter(7, x)[...]
     all_of(zo, cs, cr.at[0]).wait_send()
     all_of(rf, fs, fr).wait_send()
     all_of(ry, ys, yr.at[0]).wait_send()
-    all_of(rx.at[pl.ds(0, 3)], xs, xr).wait_recv()
-    a0 = rx[0] + rx[1]
-    a1 = rx[2] + rx[3]
+    others = all_of(rz.at[pl.ds(0, 23)], zs, zr)
+    others.wait_recv()
+
+    def total(i):
+        v = [rz[4 * k + i] for k in range(6)] + [rz[4 * k + i + 1] for k in range(6)]
+        while len(v) > 1:
+            v = [v[j] + v[j + 1] if j + 1 < len(v) else v[j] for j in range(0, len(v), 2)]
+        return v[0]
+
+    a0, a1 = total(0), total(2)
     first = jnp.concatenate([a0[:, :64], a1[:, :64]], axis=1)
     second = jnp.concatenate([a0[:, 64:], a1[:, 64:]], axis=1)
     m = jnp.concatenate([first, second], axis=0)
-    mt[...] = m.T
-    g = jnp.dot(
-        mt[pl.ds(pl.multiple_of(x * 32, 32), 32), :], m,
-        preferred_element_type=F32, precision=lax.Precision.HIGHEST,
-    )
-    for e in range(8):
+    g = jnp.dot(m.T, m, preferred_element_type=F32, precision=lax.Precision.HIGHEST)
+    for e in range(32):
         gs[e] = g[4 * e : 4 * e + 4]
 
-    own = y * 2 + c
+    place = x * 8 + y * 2 + c
 
     def to_gs(i):
-        dy, _, dc = part[i]
-        return remote(gs.at[((y + dy) & 3) * 2 + c_at[dc]], gr.at[i], gss, gsr, near(dy, 0, dc))
+        dy, dx, dc = plane[i]
+        e = ((x + dx) & 3) * 8 + ((y + dy) & 3) * 2 + c_at[dc]
+        return remote(gs.at[e], gr.at[i], gss, gsr, near(dy, dx, dc))
+
+    to_mate = remote(mx.at[x >> 1], mx.at[x >> 1], xs, xr, near(0, 2, 0))
 
     def to_gz(d):
         return remote(gz.at[z], gz.at[z], gzs, gzr, near(0, 0, 0, d))
 
-    place = x * 8 + own
-
     def to_gf(i):
         return remote(gf.at[place], gf.at[place], gfs, gfr, near(*plane[i]))
 
-    for i in range(7):
+    for i in range(31):
         to_gs(i).start()
-    ms[0, 0], ms[0, 1] = first[:16], first[16:]
-    ms[1, 0], ms[1, 1] = second[:16], second[16:]
-    both_out[128:144, :] = ms[0, xl]
-    both_out[144:160, :] = ms[1, xl]
-    all_of(rz, zs, zr).wait_send()
-    all_of(rx.at[pl.ds(0, 3)], xs, xr).wait_send()
+    mx[x >> 1] = m
+    to_mate.start()
+    others.wait_send()
     all_of(gr, gss, gsr).wait_recv()
-    gz[z] = ((gs[own] + gr[0]) + (gr[1] + gr[2])) + ((gr[3] + gr[4]) + (gr[5] + gr[6]))
+    v = [gr[i] for i in range(31)] + [gs[place]]
+    while len(v) > 1:
+        v = [v[j] + v[j + 1] for j in range(0, len(v), 2)]
+    gz[z] = v[0]
     for d in z_order:
         to_gz(d).start()
     all_of(gr, gss, gsr).wait_send()
+    to_mate.wait()
+    for i in range(2):
+        for j in range(2):
+            both_out[128 + 16 * j + 8 * i : 136 + 16 * j + 8 * i, :] = mx[i, 8 * j : 8 * j + 8]
     all_of(gz.at[pl.ds(0, 7)], gzs, gzr).wait_recv()
     gf[place] = (((gz[0] + gz[1]) + (gz[2] + gz[3])) + ((gz[4] + gz[5]) + (gz[6] + gz[7]))) * (1.0 / 4096.0)
     for i in range(31):
@@ -288,12 +294,10 @@
             V((8, 128, 128), F32),
             V((2, 128, 128), F32),
             V((6, 3, 32, 128), F32),
-            V((5, 32, 128), F32),
-            V((4, 32, 128), F32),
-            V((2, 2, 16, 128), F32),
-            V((128, 64), F32),
-            V((8, 4, 128), F32),
-            V((7, 4, 128), F32),
+            V((24, 8, 128), F32),
+            V((2, 16, 128), F32),
+            V((32, 4, 128), F32),
+            V((31, 4, 128), F32),
             V((8, 4, 128), F32),
             V((32, 4, 128), F32),
             D((9,)),
@@ -311,7 +315,7 @@
 
 
 def factor_kernel(both_ref, basis_ref, tri_ref, a_ref, u_ref):
-    n, width = 128, 32
+    n, width = 128, 64
     col = lax.axis_index("col")
     a_ref[:, :128] = both_ref[:128, :]
     samples = jnp.concatenate([both_ref[128:, :], jnp.zeros((96, 128), F32)], axis=0)

time: 46 us -> 46 us (level)
  no operation moved by 1% of the time
where the time goes in v4:
time: 46 us; the launch traced here: 45.8 us
  Pallas kernels  44.4 us (97%)
  other arithmetic  0.78 us (2%)
  between operations  0.64 us (1%)
    pallas_call x1, Pallas kernels, mix(): pl.pallas_call(mix_kernel, out_shape=jax.ShapeDtypeStruct((160, 128), F32...  39.7 us
    pallas_call x1, Pallas kernels, factor(): pl.pallas_call(factor_kernel, out_shape=(jax.ShapeDtypeStruct((32, 64), F...  4.67 us

profile of v4, /device:TPU:1, one launch (start us, length us, event | category | flops | bytes accessed | tf_op | source)
XLA Modules:
  0.0 45.8 jit_solution(187579490639993645)
XLA Ops:
  0.6 0.8 %pad_add_fusion.ints = s32[12288]{0:T(1024)S(1)} fusion(s32[4096]{0:T(1024)} %param.5, s32[8192]{0:T(1024)} %param.4), kind=kLoop, calls=%fused_computation | loop fusion | flops 12288 | bytes 98304 | tf_op jit(solution)/shard_map/concatenate | solution.py:310
  1.4 39.7 %mix.1.both_ref = f32[160,128]{1,0:T(8,128)S(1)} custom-call(f32[64,8192]{1,0:T(8,128)} %x_hbm.1, s32[12288]{0:T(1024)S(1)} %pad_add_fusion.ints), custom_call_target="tpu_custom_call" | custom-call | tf_op jit(solution)/shard_map/mix/pallas_call | solution.py:281
  41.1 4.7 %factor.1 = (f32[32,64]{1,0:T(8,128)}, f32[64,128]{1,0:T(8,128)}) custom-call(f32[160,128]{1,0:T(8,128)S(1)} %mix.1.both_ref), custom_call_target="tpu_custom_call" | custom-call | tf_op jit(solution)/shard_map/factor/pallas_call | solution.py:378

commit v5 on v4

--- a/solution.py
+++ b/solution.py
@@ -126,7 +126,7 @@
 
     left = lax.broadcasted_iota(jnp.int32, (8, 128), 1) < 64
     sub = lax.broadcasted_iota(jnp.int32, (8, 128), 0)
-    shifted = t.at[pl.ds(HALF, LOCAL)]
+    table = t.reshape(LOCAL + HALF, 1, 128)
 
     def pick(out, k, cq):
         zq = (z + away(k)) & 7
@@ -137,8 +137,8 @@
             for top in (0, 8):
                 v = None
                 for j in range(8):
-                    a = jnp.broadcast_to(t[pl.ds(idx[q * 32 + top + j], 1), :], (8, 128))
-                    b = jnp.broadcast_to(shifted[pl.ds(idx[q * 32 + 16 + top + j], 1), :], (8, 128))
+                    a = jnp.broadcast_to(table[idx[q * 32 + top + j]], (8, 128))
+                    b = jnp.broadcast_to(table[idx[q * 32 + 16 + top + j] + HALF], (8, 128))
                     r = jnp.where(left, a, b)
                     v = r if v is None else jnp.where(sub == j, r, v)
                 out[k, pl.ds(pl.multiple_of(i * 16, 16) + top, 8), :] = v * sign
@@ -315,7 +315,7 @@
 
 
 def factor_kernel(both_ref, basis_ref, tri_ref, a_ref, u_ref):
-    n, width = 128, 64
+    n, width = 128, 32
     col = lax.axis_index("col")
     a_ref[:, :128] = both_ref[:128, :]
     samples = jnp.concatenate([both_ref[128:, :], jnp.zeros((96, 128), F32)], axis=0)
@@ -365,8 +365,13 @@
         if top + width < n:
             rest = top + width
             u = u_ref[top:rest, :]
-            left = u[:, :128].T[rest:, :]
-            upd = jnp.dot(left, u, preferred_element_type=F32, precision=lax.Precision.HIGHEST)
+            hi = u.astype(BF16)
+            low = u - hi.astype(F32)
+            mid = low.astype(BF16)
+            low = (low - mid.astype(F32)).astype(BF16)
+            left = jnp.concatenate([v[:, :128] for v in (hi, hi, mid, hi, low, mid)], axis=0)
+            right = jnp.concatenate([hi, mid, hi, low, hi, mid], axis=0)
+            upd = jnp.dot(left.T[rest:, :], right, preferred_element_type=F32)
             a_ref[rest:, :] = a_ref[rest:, :] - upd
     half = pl.ds(pl.multiple_of(col * 64, 64), 64)
     tri_ref[...] = u_ref[half, :128]

time: 46 us -> 45.8 us (level)
  no operation moved by 1% of the time
where the time goes in v5:
time: 45.8 us; the launch traced here: 45.6 us
  Pallas kernels  44.2 us (97%)
  other arithmetic  0.78 us (2%)
  between operations  0.64 us (1%)
    pallas_call x1, Pallas kernels, mix(): pl.pallas_call(mix_kernel, out_shape=jax.ShapeDtypeStruct((160, 128), F32...  39.7 us
    pallas_call x1, Pallas kernels, factor(): pl.pallas_call(factor_kernel, out_shape=(jax.ShapeDtypeStruct((32, 64), F...  4.44 us

profile of v5, /device:TPU:1, one launch (start us, length us, event | category | flops | bytes accessed | tf_op | source)
XLA Modules:
  0.0 45.6 jit_solution(6657231889102135872)
XLA Ops:
  0.6 0.8 %pad_add_fusion.ints = s32[12288]{0:T(1024)S(1)} fusion(s32[4096]{0:T(1024)} %param.5, s32[8192]{0:T(1024)} %param.4), kind=kLoop, calls=%fused_computation | loop fusion | flops 12288 | bytes 98304 | tf_op jit(solution)/shard_map/concatenate | solution.py:310
  1.4 39.7 %mix.1.both_ref = f32[160,128]{1,0:T(8,128)S(1)} custom-call(f32[64,8192]{1,0:T(8,128)} %x_hbm.1, s32[12288]{0:T(1024)S(1)} %pad_add_fusion.ints), custom_call_target="tpu_custom_call" | custom-call | tf_op jit(solution)/shard_map/mix/pallas_call | solution.py:281
  41.1 4.4 %factor.1 = (f32[32,64]{1,0:T(8,128)}, f32[64,128]{1,0:T(8,128)}) custom-call(f32[160,128]{1,0:T(8,128)S(1)} %mix.1.both_ref), custom_call_target="tpu_custom_call" | custom-call | tf_op jit(solution)/shard_map/factor/pallas_call | solution.py:383

commit v6 on v5

--- a/solution.py
+++ b/solution.py
@@ -124,8 +124,7 @@
     place_rows.wait()
     pl.semaphore_wait(barrier, 53)
 
-    left = lax.broadcasted_iota(jnp.int32, (8, 128), 1) < 64
-    sub = lax.broadcasted_iota(jnp.int32, (8, 128), 0)
+    left = lax.broadcasted_iota(jnp.int32, (1, 128), 1) < 64
     table = t.reshape(LOCAL + HALF, 1, 128)
 
     def pick(out, k, cq):
@@ -134,14 +133,10 @@
         def body(i, carry):
             q = zq * 16 + i * 2 + cq
             sign = (1 - 2 * parity(row & q)).astype(F32)
-            for top in (0, 8):
-                v = None
-                for j in range(8):
-                    a = jnp.broadcast_to(table[idx[q * 32 + top + j]], (8, 128))
-                    b = jnp.broadcast_to(table[idx[q * 32 + 16 + top + j] + HALF], (8, 128))
-                    r = jnp.where(left, a, b)
-                    v = r if v is None else jnp.where(sub == j, r, v)
-                out[k, pl.ds(pl.multiple_of(i * 16, 16) + top, 8), :] = v * sign
+            for j in range(16):
+                a = table[idx[q * 32 + j]]
+                b = table[idx[q * 32 + 16 + j] + HALF]
+                out[k, pl.ds(pl.multiple_of(i * 16, 16) + j, 1), :] = jnp.where(left, a, b) * sign
             return carry
 
         lax.fori_loop(0, 8, body, 0, unroll=8)

time: 45.8 us -> 45.7 us (level)
  no operation moved by 1% of the time
where the time goes in v6:
time: 45.7 us; the launch traced here: 45.6 us
  Pallas kernels  44.1 us (96%)
  other arithmetic  0.78 us (2%)
  between operations  0.64 us (1%)
    pallas_call x1, Pallas kernels, mix(): pl.pallas_call(mix_kernel, out_shape=jax.ShapeDtypeStruct((160, 128), F32...  39.7 us
    pallas_call x1, Pallas kernels, factor(): pl.pallas_call(factor_kernel, out_shape=(jax.ShapeDtypeStruct((32, 64), F...  4.44 us

profile of v6, /device:TPU:1, one launch (start us, length us, event | category | flops | bytes accessed | tf_op | source)
XLA Modules:
  0.0 45.6 jit_solution(8573402433838155851)
XLA Ops:
  0.6 0.8 %pad_add_fusion.ints = s32[12288]{0:T(1024)S(1)} fusion(s32[4096]{0:T(1024)} %param.5, s32[8192]{0:T(1024)} %param.4), kind=kLoop, calls=%fused_computation | loop fusion | flops 12288 | bytes 98304 | tf_op jit(solution)/shard_map/concatenate | solution.py:305
  1.4 39.7 %mix.1.both_ref = f32[160,128]{1,0:T(8,128)S(1)} custom-call(f32[64,8192]{1,0:T(8,128)} %x_hbm.1, s32[12288]{0:T(1024)S(1)} %pad_add_fusion.ints), custom_call_target="tpu_custom_call" | custom-call | tf_op jit(solution)/shard_map/mix/pallas_call | solution.py:276
  41.1 4.4 %factor.1 = (f32[32,64]{1,0:T(8,128)}, f32[64,128]{1,0:T(8,128)}) custom-call(f32[160,128]{1,0:T(8,128)S(1)} %mix.1.both_ref), custom_call_target="tpu_custom_call" | custom-call | tf_op jit(solution)/shard_map/factor/pallas_call | solution.py:378

commit v7 on v5

--- a/solution.py
+++ b/solution.py
@@ -19,6 +19,13 @@
     bits = bits ^ (bits >> 2)
     bits = bits ^ (bits >> 1)
     return bits & 1
+
+
+def split(v):
+    hi = v.astype(BF16)
+    rest = v - hi.astype(F32)
+    mid = rest.astype(BF16)
+    return hi, mid, (rest - mid.astype(F32)).astype(BF16)
 
 
 def away(k):
@@ -104,11 +111,7 @@
             for top in (0, NU // 2):
                 at = (2 * g + i + top) * LO
                 v = xv[:, at : at + LO]
-                hi = v.astype(BF16)
-                rest = v - hi.astype(F32)
-                mid = rest.astype(BF16)
-                low = (rest - mid.astype(F32)).astype(BF16)
-                parts.append(jnp.concatenate([hi, mid, low], axis=1))
+                parts.append(jnp.concatenate(split(v), axis=1))
         w = jnp.concatenate(parts, axis=0)
         o = lax.dot_general(h, w, (((1,), (1,)), ((), ())), preferred_element_type=F32)
         for i in range(2):
@@ -226,7 +229,9 @@
     first = jnp.concatenate([a0[:, :64], a1[:, :64]], axis=1)
     second = jnp.concatenate([a0[:, 64:], a1[:, 64:]], axis=1)
     m = jnp.concatenate([first, second], axis=0)
-    g = jnp.dot(m.T, m, preferred_element_type=F32, precision=lax.Precision.HIGHEST)
+    hi, mid, low = split(m)
+    deep = jnp.concatenate([hi, hi, mid, hi, low, mid], axis=0)
+    g = jnp.dot(deep.T, jnp.concatenate([hi, mid, hi, low, hi, mid], axis=0), preferred_element_type=F32)
     for e in range(32):
         gs[e] = g[4 * e : 4 * e + 4]
 
@@ -314,7 +319,7 @@
     return jnp.broadcast_to(v[:, j : j + 1], (8, 128))
 
 
-def factor_kernel(both_ref, basis_ref, tri_ref, a_ref, u_ref):
+def factor_kernel(both_ref, basis_ref, tri_ref, a_ref, u_ref, p_ref):
     n, width = 128, 32
     col = lax.axis_index("col")
     a_ref[:, :128] = both_ref[:128, :]
@@ -330,10 +335,9 @@
         ]
         for j in range(nb):
             at = top + 8 * j
-            rows = [
-                [jnp.broadcast_to(blocks[j][t][k : k + 1, :], (8, 128)) for t in range(2)]
-                for k in range(8)
-            ]
+            for i in range(2):
+                p_ref[2 * at + 8 * i : 2 * at + 8 * i + 8, :] = blocks[j][i]
+            rows = [[p_ref[pl.ds(2 * at + 8 * i + k, 8, stride=0), :] for i in range(2)] for k in range(8)]
             d = {(i, k): rows_const(rows[i][0], at + k) for i in range(8) for k in range(i + 1)}
             below = [[rows_const(blocks[i][0], at + k) for k in range(8)] for i in range(j + 1, nb)]
             for k in range(8):
@@ -365,10 +369,7 @@
         if top + width < n:
             rest = top + width
             u = u_ref[top:rest, :]
-            hi = u.astype(BF16)
-            low = u - hi.astype(F32)
-            mid = low.astype(BF16)
-            low = (low - mid.astype(F32)).astype(BF16)
+            hi, mid, low = split(u)
             left = jnp.concatenate([v[:, :128] for v in (hi, hi, mid, hi, low, mid)], axis=0)
             right = jnp.concatenate([hi, mid, hi, low, hi, mid], axis=0)
             upd = jnp.dot(left.T[rest:, :], right, preferred_element_type=F32)
@@ -385,7 +386,7 @@
         out_shape=(jax.ShapeDtypeStruct((32, 64), F32), jax.ShapeDtypeStruct((64, 128), F32)),
         in_specs=[vm],
         out_specs=(vm, vm),
-        scratch_shapes=[pltpu.VMEM((128, 256), F32), pltpu.VMEM((128, 256), F32)],
+        scratch_shapes=[pltpu.VMEM((128, 256), F32), pltpu.VMEM((128, 256), F32), pltpu.VMEM((256, 128), F32)],
         compiler_params=pltpu.CompilerParams(vmem_limit_bytes=16 << 20),
         name="factor",
     )(both)

time: 45.8 us -> 45.2 us (0.987)
  Pallas kernels: 44.2 us -> 43.6 us
where the time goes in v7:
time: 45.2 us; the launch traced here: 45 us
  Pallas kernels  43.6 us (96%)
  other arithmetic  0.78 us (2%)
  between operations  0.64 us (1%)
    pallas_call x1, Pallas kernels, mix(): pl.pallas_call(mix_kernel, out_shape=jax.ShapeDtypeStruct((160, 128), F32...  39.6 us
    pallas_call x1, Pallas kernels, factor(): pl.pallas_call(factor_kernel, out_shape=(jax.ShapeDtypeStruct((32, 64), F...  3.99 us

profile of v7, /device:TPU:1, one launch (start us, length us, event | category | flops | bytes accessed | tf_op | source)
XLA Modules:
  0.0 45.0 jit_solution(10858893314398876490)
XLA Ops:
  0.6 0.8 %pad_add_fusion.ints = s32[12288]{0:T(1024)S(1)} fusion(s32[4096]{0:T(1024)} %param.5, s32[8192]{0:T(1024)} %param.4), kind=kLoop, calls=%fused_computation | loop fusion | flops 12288 | bytes 98304 | tf_op jit(solution)/shard_map/concatenate | solution.py:315
  1.4 39.6 %mix.1.both_ref = f32[160,128]{1,0:T(8,128)S(1)} custom-call(f32[64,8192]{1,0:T(8,128)} %x_hbm.1, s32[12288]{0:T(1024)S(1)} %pad_add_fusion.ints), custom_call_target="tpu_custom_call" | custom-call | tf_op jit(solution)/shard_map/mix/pallas_call | solution.py:286
  41.0 4.0 %factor.1 = (f32[32,64]{1,0:T(8,128)}, f32[64,128]{1,0:T(8,128)}) custom-call(f32[160,128]{1,0:T(8,128)S(1)} %mix.1.both_ref), custom_call_target="tpu_custom_call" | custom-call | tf_op jit(solution)/shard_map/factor/pallas_call | solution.py:384

commit v8 on v7

--- a/solution.py
+++ b/solution.py
@@ -74,7 +74,9 @@
     loop(0, 8, lambda i: fetch(i).start())
     idxv[...] = ints[pl.ds(LOCAL, 4096)] & (LOCAL - 1)
     place_rows.start()
-    sgv[...] = ints[pl.ds(0, LOCAL)].reshape(LOCAL // 128, 128).astype(F32)
+    signs = ints[pl.ds(0, LOCAL)].reshape(LOCAL // 128, 128).astype(F32)
+    for i in range(LOCAL // 128):
+        sgv[8 * i : 8 * i + 8, :] = jnp.broadcast_to(signs[i : i + 1, :], (8, 128))
 
     barrier = pltpu.get_barrier_semaphore()
     for d in [near(*i) for i in plane] + [near(0, i, 0, d) for d in z_order for i in range(4 if 1 < d < 7 else 1)]:
@@ -92,7 +94,7 @@
             v = []
             for u in range(NU):
                 at = u * LO + bt * 128
-                v.append(xv[rows, at : at + 128] * sgv[at // 128 : at // 128 + 1, :])
+                v.append(xv[rows, at : at + 128] * sgv[at // 16 : at // 16 + 8, :])
             step = 1
             while step < NU:
                 for u in range(NU):
@@ -264,9 +266,8 @@
         to_gz(d).start()
     all_of(gr, gss, gsr).wait_send()
     to_mate.wait()
-    for i in range(2):
-        for j in range(2):
-            both_out[128 + 16 * j + 8 * i : 136 + 16 * j + 8 * i, :] = mx[i, 8 * j : 8 * j + 8]
+    quarters = [mx[i, 8 * j : 8 * j + 8] for j in range(2) for i in range(2)]
+    both_out[:, 128:] = jnp.concatenate(quarters + [jnp.zeros((96, 128), F32)], axis=0).T
     all_of(gz.at[pl.ds(0, 7)], gzs, gzr).wait_recv()
     gf[place] = (((gz[0] + gz[1]) + (gz[2] + gz[3])) + ((gz[4] + gz[5]) + (gz[6] + gz[7]))) * (1.0 / 4096.0)
     for i in range(31):
@@ -274,7 +275,7 @@
     all_of(gz.at[pl.ds(0, 7)], gzs, gzr).wait_send()
     all_of(gf.at[pl.ds(0, 31)], gfs, gfr).wait_recv()
     for e in range(32):
-        both_out[e * 4 : (e + 1) * 4, :] = gf[e]
+        both_out[e * 4 : (e + 1) * 4, :128] = gf[e]
     all_of(gf.at[pl.ds(0, 31)], gfs, gfr).wait_send()
 
 
@@ -285,12 +286,12 @@
     D = pltpu.SemaphoreType.DMA
     return pl.pallas_call(
         mix_kernel,
-        out_shape=jax.ShapeDtypeStruct((160, 128), F32),
+        out_shape=jax.ShapeDtypeStruct((128, 256), F32),
         in_specs=[hbm, vm],
         out_specs=vm,
         scratch_shapes=[
             V((64, LOCAL), F32),
-            V((LOCAL // 128, 128), F32),
+            V((LOCAL // 16, 128), F32),
             V((4096,), jnp.int32),
             pltpu.SMEM((4096,), jnp.int32),
             V((LOCAL + HALF, 128), F32),
@@ -322,15 +323,13 @@
 def factor_kernel(both_ref, basis_ref, tri_ref, a_ref, u_ref, p_ref):
     n, width = 128, 32
     col = lax.axis_index("col")
-    a_ref[:, :128] = both_ref[:128, :]
-    samples = jnp.concatenate([both_ref[128:, :], jnp.zeros((96, 128), F32)], axis=0)
-    a_ref[:, 128:] = samples.T
     lane = lax.broadcasted_iota(jnp.int32, (8, 128), 1)
     for panel in range(n // width):
         top = panel * width
         nb = width // 8
+        source = a_ref if panel else both_ref
         blocks = [
-            [a_ref[top + 8 * i : top + 8 * i + 8, 128 * t : 128 * t + 128] for t in range(2)]
+            [source[top + 8 * i : top + 8 * i + 8, 128 * t : 128 * t + 128] for t in range(2)]
             for i in range(nb)
         ]
         for j in range(nb):
@@ -373,7 +372,7 @@
             left = jnp.concatenate([v[:, :128] for v in (hi, hi, mid, hi, low, mid)], axis=0)
             right = jnp.concatenate([hi, mid, hi, low, hi, mid], axis=0)
             upd = jnp.dot(left.T[rest:, :], right, preferred_element_type=F32)
-            a_ref[rest:, :] = a_ref[rest:, :] - upd
+            a_ref[rest:, :] = source[rest:, :] - upd
     half = pl.ds(pl.multiple_of(col * 64, 64), 64)
     tri_ref[...] = u_ref[half, :128]
     basis_ref[...] = u_ref[half, 128:].T[:32]

time: 45.2 us -> 45.2 us (level)
  no operation moved by 1% of the time
where the time goes in v8:
time: 45.2 us; the launch traced here: 45 us
  Pallas kernels  43.6 us (96%)
  other arithmetic  0.78 us (2%)
  between operations  0.64 us (1%)
    pallas_call x1, Pallas kernels, mix(): pl.pallas_call(mix_kernel, out_shape=jax.ShapeDtypeStruct((128, 256), F32...  39.6 us
    pallas_call x1, Pallas kernels, factor(): pl.pallas_call(factor_kernel, out_shape=(jax.ShapeDtypeStruct((32, 64), F...  3.98 us

profile of v8, /device:TPU:1, one launch (start us, length us, event | category | flops | bytes accessed | tf_op | source)
XLA Modules:
  0.0 45.0 jit_solution(337687437111098299)
XLA Ops:
  0.6 0.8 %pad_add_fusion.ints = s32[12288]{0:T(1024)S(1)} fusion(s32[4096]{0:T(1024)} %param.5, s32[8192]{0:T(1024)} %param.4), kind=kLoop, calls=%fused_computation | loop fusion | flops 12288 | bytes 98304 | tf_op jit(solution)/shard_map/concatenate | solution.py:316
  1.4 39.6 %mix.1.both_ref = f32[128,256]{1,0:T(8,128)S(1)} custom-call(f32[64,8192]{1,0:T(8,128)} %x_hbm.1, s32[12288]{0:T(1024)S(1)} %pad_add_fusion.ints), custom_call_target="tpu_custom_call" | custom-call | tf_op jit(solution)/shard_map/mix/pallas_call | solution.py:287
  41.0 4.0 %factor.1 = (f32[32,64]{1,0:T(8,128)}, f32[64,128]{1,0:T(8,128)}) custom-call(f32[128,256]{1,0:T(8,128)S(1)} %mix.1.both_ref), custom_call_target="tpu_custom_call" | custom-call | tf_op jit(solution)/shard_map/factor/pallas_call | solution.py:383

commit v9 on v7

--- a/solution.py
+++ b/solution.py
@@ -77,9 +77,10 @@
     sgv[...] = ints[pl.ds(0, LOCAL)].reshape(LOCAL // 128, 128).astype(F32)
 
     barrier = pltpu.get_barrier_semaphore()
-    for d in [near(*i) for i in plane] + [near(0, i, 0, d) for d in z_order for i in range(4 if 1 < d < 7 else 1)]:
-        pl.semaphore_signal(barrier, inc=1, device_id=d, device_id_type=MESH)
-
+    early = [(0, 0, 1, 0), (0, 0, 0, 1), (0, 0, 0, 7)] + [(d, 0, 0, 0) for d in (2, 1, 3)]
+    early += [(0, i, 0, d) for d in (4, 3, 5, 2, 6, 0) for i in range(4) if d or i]
+    for at in early:
+        pl.semaphore_signal(barrier, inc=1, device_id=near(*at), device_id_type=MESH)
     ri = lax.broadcasted_iota(jnp.int32, (LO, LO), 0)
     ci = lax.broadcasted_iota(jnp.int32, (LO, LO), 1)
     h = ((1 - 2 * parity(ri & ci)).astype(F32) * (1.0 / 1024.0)).astype(BF16)
@@ -125,7 +126,7 @@
         lower(g)
 
     place_rows.wait()
-    pl.semaphore_wait(barrier, 53)
+    pl.semaphore_wait(barrier, len(early))
 
     left = lax.broadcasted_iota(jnp.int32, (8, 128), 1) < 64
     sub = lax.broadcasted_iota(jnp.int32, (8, 128), 0)

time: 45.2 us -> 44.9 us (level)
  no operation moved by 1% of the time
where the time goes in v9:
time: 44.9 us; the launch traced here: 44.7 us
  Pallas kernels  43.3 us (96%)
  other arithmetic  0.78 us (2%)
  between operations  0.64 us (1%)
    pallas_call x1, Pallas kernels, mix(): pl.pallas_call(mix_kernel, out_shape=jax.ShapeDtypeStruct((160, 128), F32...  39.3 us
    pallas_call x1, Pallas kernels, factor(): pl.pallas_call(factor_kernel, out_shape=(jax.ShapeDtypeStruct((32, 64), F...  4 us

profile of v9, /device:TPU:1, one launch (start us, length us, event | category | flops | bytes accessed | tf_op | source)
XLA Modules:
  0.0 44.7 jit_solution(11284532238034823594)
XLA Ops:
  0.6 0.8 %pad_add_fusion.ints = s32[12288]{0:T(1024)S(1)} fusion(s32[4096]{0:T(1024)} %param.5, s32[8192]{0:T(1024)} %param.4), kind=kLoop, calls=%fused_computation | loop fusion | flops 12288 | bytes 98304 | tf_op jit(solution)/shard_map/concatenate | solution.py:316
  1.4 39.3 %mix.1.both_ref = f32[160,128]{1,0:T(8,128)S(1)} custom-call(f32[64,8192]{1,0:T(8,128)} %x_hbm.1, s32[12288]{0:T(1024)S(1)} %pad_add_fusion.ints), custom_call_target="tpu_custom_call" | custom-call | tf_op jit(solution)/shard_map/mix/pallas_call | solution.py:287
  40.7 4.0 %factor.1 = (f32[32,64]{1,0:T(8,128)}, f32[64,128]{1,0:T(8,128)}) custom-call(f32[160,128]{1,0:T(8,128)S(1)} %mix.1.both_ref), custom_call_target="tpu_custom_call" | custom-call | tf_op jit(solution)/shard_map/factor/pallas_call | solution.py:385

commit v10 on v9

--- a/solution.py
+++ b/solution.py
@@ -320,7 +320,7 @@
     return jnp.broadcast_to(v[:, j : j + 1], (8, 128))
 
 
-def factor_kernel(both_ref, basis_ref, tri_ref, a_ref, u_ref, p_ref):
+def factor_kernel(both_ref, basis_ref, tri_ref, a_ref, u_ref, p_ref, q_ref):
     n, width = 128, 32
     col = lax.axis_index("col")
     a_ref[:, :128] = both_ref[:128, :]
@@ -339,7 +339,9 @@
             for i in range(2):
                 p_ref[2 * at + 8 * i : 2 * at + 8 * i + 8, :] = blocks[j][i]
             rows = [[p_ref[pl.ds(2 * at + 8 * i + k, 8, stride=0), :] for i in range(2)] for k in range(8)]
-            d = {(i, k): rows_const(rows[i][0], at + k) for i in range(8) for k in range(i + 1)}
+            for k in range(8):
+                q_ref[8 * (at + k) : 8 * (at + k) + 8, :] = rows_const(blocks[j][0], at + k)
+            d = {(i, k): q_ref[pl.ds(8 * (at + k) + i, 8, stride=0), :] for i in range(8) for k in range(i + 1)}
             below = [[rows_const(blocks[i][0], at + k) for k in range(8)] for i in range(j + 1, nb)]
             for k in range(8):
                 r = lax.rsqrt(d[k, k])
@@ -387,7 +389,7 @@
         out_shape=(jax.ShapeDtypeStruct((32, 64), F32), jax.ShapeDtypeStruct((64, 128), F32)),
         in_specs=[vm],
         out_specs=(vm, vm),
-        scratch_shapes=[pltpu.VMEM((128, 256), F32), pltpu.VMEM((128, 256), F32), pltpu.VMEM((256, 128), F32)],
+        scratch_shapes=[pltpu.VMEM((128, 256), F32), pltpu.VMEM((128, 256), F32), pltpu.VMEM((256, 128), F32), pltpu.VMEM((1024, 128), F32)],
         compiler_params=pltpu.CompilerParams(vmem_limit_bytes=16 << 20),
         name="factor",
     )(both)

time: 44.9 us -> 44.8 us (level)
  no operation moved by 1% of the time
where the time goes in v10:
time: 44.8 us; the launch traced here: 44.7 us
  Pallas kernels  43.2 us (96%)
  other arithmetic  0.78 us (2%)
  between operations  0.64 us (1%)
    pallas_call x1, Pallas kernels, mix(): pl.pallas_call(mix_kernel, out_shape=jax.ShapeDtypeStruct((160, 128), F32...  39.3 us
    pallas_call x1, Pallas kernels, factor(): pl.pallas_call(factor_kernel, out_shape=(jax.ShapeDtypeStruct((32, 64), F...  3.92 us

profile of v10, /device:TPU:1, one launch (start us, length us, event | category | flops | bytes accessed | tf_op | source)
XLA Modules:
  0.0 44.7 jit_solution(17950944759214086157)
XLA Ops:
  0.6 0.8 %pad_add_fusion.ints = s32[12288]{0:T(1024)S(1)} fusion(s32[4096]{0:T(1024)} %param.5, s32[8192]{0:T(1024)} %param.4), kind=kLoop, calls=%fused_computation | loop fusion | flops 12288 | bytes 98304 | tf_op jit(solution)/shard_map/concatenate | solution.py:316
  1.4 39.3 %mix.1.both_ref = f32[160,128]{1,0:T(8,128)S(1)} custom-call(f32[64,8192]{1,0:T(8,128)} %x_hbm.1, s32[12288]{0:T(1024)S(1)} %pad_add_fusion.ints), custom_call_target="tpu_custom_call" | custom-call | tf_op jit(solution)/shard_map/mix/pallas_call | solution.py:287
  40.7 3.9 %factor.1 = (f32[32,64]{1,0:T(8,128)}, f32[64,128]{1,0:T(8,128)}) custom-call(f32[160,128]{1,0:T(8,128)S(1)} %mix.1.both_ref), custom_call_target="tpu_custom_call" | custom-call | tf_op jit(solution)/shard_map/factor/pallas_call | solution.py:387

commit v11 on v10

--- a/solution.py
+++ b/solution.py
@@ -72,7 +72,8 @@
         return pltpu.make_async_copy(x_hbm.at[at], xv.at[at], in_sem.at[i])
 
     loop(0, 8, lambda i: fetch(i).start())
-    idxv[...] = ints[pl.ds(LOCAL, 4096)] & (LOCAL - 1)
+    picks = (ints[pl.ds(LOCAL, 4096)] & (LOCAL - 1)).reshape(32, 128)
+    idxv[...] = (picks | ((pltpu.roll(picks, 112, 1) + HALF) << 14)).reshape(4096)
     place_rows.start()
     sgv[...] = ints[pl.ds(0, LOCAL)].reshape(LOCAL // 128, 128).astype(F32)
 
@@ -141,8 +142,9 @@
             for top in (0, 8):
                 v = None
                 for j in range(8):
-                    a = jnp.broadcast_to(table[idx[q * 32 + top + j]], (8, 128))
-                    b = jnp.broadcast_to(table[idx[q * 32 + 16 + top + j] + HALF], (8, 128))
+                    both = idx[q * 32 + top + j]
+                    a = jnp.broadcast_to(table[both & 16383], (8, 128))
+                    b = jnp.broadcast_to(table[both >> 14], (8, 128))
                     r = jnp.where(left, a, b)
                     v = r if v is None else jnp.where(sub == j, r, v)
                 out[k, pl.ds(pl.multiple_of(i * 16, 16) + top, 8), :] = v * sign

time: 44.8 us -> 44.9 us (level)
  no operation moved by 1% of the time
where the time goes in v11:
time: 44.9 us; the launch traced here: 44.7 us
  Pallas kernels  43.3 us (96%)
  other arithmetic  0.78 us (2%)
  between operations  0.64 us (1%)
    pallas_call x1, Pallas kernels, mix(): pl.pallas_call(mix_kernel, out_shape=jax.ShapeDtypeStruct((160, 128), F32...  39.3 us
    pallas_call x1, Pallas kernels, factor(): pl.pallas_call(factor_kernel, out_shape=(jax.ShapeDtypeStruct((32, 64), F...  3.92 us

profile of v11, /device:TPU:1, one launch (start us, length us, event | category | flops | bytes accessed | tf_op | source)
XLA Modules:
  0.0 44.7 jit_solution(17508049913911851206)
XLA Ops:
  0.6 0.8 %pad_add_fusion.ints = s32[12288]{0:T(1024)S(1)} fusion(s32[4096]{0:T(1024)} %param.5, s32[8192]{0:T(1024)} %param.4), kind=kLoop, calls=%fused_computation | loop fusion | flops 12288 | bytes 98304 | tf_op jit(solution)/shard_map/concatenate | solution.py:318
  1.4 39.3 %mix.1.both_ref = f32[160,128]{1,0:T(8,128)S(1)} custom-call(f32[64,8192]{1,0:T(8,128)} %x_hbm.1, s32[12288]{0:T(1024)S(1)} %pad_add_fusion.ints), custom_call_target="tpu_custom_call" | custom-call | tf_op jit(solution)/shard_map/mix/pallas_call | solution.py:289
  40.7 3.9 %factor.1 = (f32[32,64]{1,0:T(8,128)}, f32[64,128]{1,0:T(8,128)}) custom-call(f32[160,128]{1,0:T(8,128)S(1)} %mix.1.both_ref), custom_call_target="tpu_custom_call" | custom-call | tf_op jit(solution)/shard_map/factor/pallas_call | solution.py:389

commit v12 on v10

--- a/solution.py
+++ b/solution.py
@@ -206,10 +206,11 @@
 
     loop(0, 8, pick_other)
     loop(0, 8, pick_own)
+    loop(2, 4, pass_z)
     all_of(rf, fs, fr).wait_recv()
     acc[7] = acc[7] + (rf[0] + rf[1])
     send_y(7)
-    loop(2, 7, pass_z)
+    loop(4, 7, pass_z)
     add_y(7)
     for d in (2, 1, 3):
         to_z(7, z, d).start()

time: 44.8 us -> 44.8 us (level)
  no operation moved by 1% of the time
where the time goes in v12:
time: 44.8 us; the launch traced here: 44.6 us
  Pallas kernels  43.2 us (96%)
  other arithmetic  0.78 us (2%)
  between operations  0.64 us (1%)
    pallas_call x1, Pallas kernels, mix(): pl.pallas_call(mix_kernel, out_shape=jax.ShapeDtypeStruct((160, 128), F32...  39.2 us
    pallas_call x1, Pallas kernels, factor(): pl.pallas_call(factor_kernel, out_shape=(jax.ShapeDtypeStruct((32, 64), F...  3.92 us

profile of v12, /device:TPU:1, one launch (start us, length us, event | category | flops | bytes accessed | tf_op | source)
XLA Modules:
  0.0 44.6 jit_solution(16446624216787228094)
XLA Ops:
  0.6 0.8 %pad_add_fusion.ints = s32[12288]{0:T(1024)S(1)} fusion(s32[4096]{0:T(1024)} %param.5, s32[8192]{0:T(1024)} %param.4), kind=kLoop, calls=%fused_computation | loop fusion | flops 12288 | bytes 98304 | tf_op jit(solution)/shard_map/concatenate | solution.py:317
  1.4 39.2 %mix.1.both_ref = f32[160,128]{1,0:T(8,128)S(1)} custom-call(f32[64,8192]{1,0:T(8,128)} %x_hbm.1, s32[12288]{0:T(1024)S(1)} %pad_add_fusion.ints), custom_call_target="tpu_custom_call" | custom-call | tf_op jit(solution)/shard_map/mix/pallas_call | solution.py:288
  40.7 3.9 %factor.1 = (f32[32,64]{1,0:T(8,128)}, f32[64,128]{1,0:T(8,128)}) custom-call(f32[160,128]{1,0:T(8,128)S(1)} %mix.1.both_ref), custom_call_target="tpu_custom_call" | custom-call | tf_op jit(solution)/shard_map/factor/pallas_call | solution.py:388

commit v13 on v10

--- a/solution.py
+++ b/solution.py
@@ -209,7 +209,8 @@
     all_of(rf, fs, fr).wait_recv()
     acc[7] = acc[7] + (rf[0] + rf[1])
     send_y(7)
-    loop(2, 7, pass_z)
+    for k in range(2, 7):
+        pass_z(k)
     add_y(7)
     for d in (2, 1, 3):
         to_z(7, z, d).start()

time: 44.8 us -> 44.8 us (level)
  no operation moved by 1% of the time
where the time goes in v13:
time: 44.8 us; the launch traced here: 44.7 us
  Pallas kernels  43.2 us (96%)
  other arithmetic  0.78 us (2%)
  between operations  0.64 us (1%)
    pallas_call x1, Pallas kernels, mix(): pl.pallas_call(mix_kernel, out_shape=jax.ShapeDtypeStruct((160, 128), F32...  39.3 us
    pallas_call x1, Pallas kernels, factor(): pl.pallas_call(factor_kernel, out_shape=(jax.ShapeDtypeStruct((32, 64), F...  3.92 us

profile of v13, /device:TPU:1, one launch (start us, length us, event | category | flops | bytes accessed | tf_op | source)
XLA Modules:
  0.0 44.7 jit_solution(3775924505209061693)
XLA Ops:
  0.6 0.8 %pad_add_fusion.ints = s32[12288]{0:T(1024)S(1)} fusion(s32[4096]{0:T(1024)} %param.5, s32[8192]{0:T(1024)} %param.4), kind=kLoop, calls=%fused_computation | loop fusion | flops 12288 | bytes 98304 | tf_op jit(solution)/shard_map/concatenate | solution.py:317
  1.4 39.3 %mix.1.both_ref = f32[160,128]{1,0:T(8,128)S(1)} custom-call(f32[64,8192]{1,0:T(8,128)} %x_hbm.1, s32[12288]{0:T(1024)S(1)} %pad_add_fusion.ints), custom_call_target="tpu_custom_call" | custom-call | tf_op jit(solution)/shard_map/mix/pallas_call | solution.py:288
  40.7 3.9 %factor.1 = (f32[32,64]{1,0:T(8,128)}, f32[64,128]{1,0:T(8,128)}) custom-call(f32[160,128]{1,0:T(8,128)S(1)} %mix.1.both_ref), custom_call_target="tpu_custom_call" | custom-call | tf_op jit(solution)/shard_map/factor/pallas_call | solution.py:388
